TPU v7x, 32 devices: a whole 2x2x4 slice. The times are simulated.
32 devices in a mesh: tok: 32 (over z, y, x, core), tp: 1.
Axes of the slice: x: 2, y: 2, z: 4, core: 2. Of those that a mesh axis runs over, the one named last changes fastest.
Arguments:
- tokens: bfloat16 [4096, 4096], P('tok', 'tp'), may hold values from -6 to 6
- w_query: bfloat16 [4096, 4096], P('tok', 'tp'), may hold values from -0.09375 to 0.09375
- w_key: bfloat16 [4096, 4096], P('tok', 'tp'), may hold values from -0.09375 to 0.09375
- w_value: bfloat16 [4096, 4096], P('tok', 'tp'), may hold values from -0.09375 to 0.09375
- short_taps: float32 [3, 3, 4096], P(None, None, 'tp'), may hold values from -3.5 to 3.5
- filters: float32 [4096, 4096], P(('tp', 'tok')), may hold values from -90 to 90, as said below
- skip_gain: float32 [4096], P(('tp', 'tok')), may hold values from 0.1 to 1.9
Outputs:
- layer_out: bfloat16 [4096, 4096], P('tok', 'tp')
Inputs may be any that keep to these rules, and one draw needn't show every extreme that they name: `filters`: real-valued filter taps.
All inputs are finite; a program needn't handle non-finite values.
Results may differ from a plain program's by a relative error of at most 0.009.
Values may be sent and summed in bfloat16 or wider, within the bound.
A program may use at most 192 MiB of HBM per device.

v0:
```python
import math

import jax
import jax.numpy as jnp
from jax import lax
from jax.sharding import PartitionSpec as P


def passed_along(value, axis, steps):
    count = lax.axis_size(axis)
    leading, last = (max(0, -steps), min(count, count - steps))
    return lax.ppermute(value, axis, [(source, source + steps) for source in range(leading, last)])


def split_lengths(length):
    inner = 1
    divisor = 1
    while divisor * divisor <= length:
        if length % divisor == 0:
            inner = divisor
        divisor += 1
    return (2 * length // inner, inner)


def angle_table(rows_count, cols_count, period):
    product = lax.broadcasted_iota(jnp.int32, (rows_count, cols_count), 0) * lax.broadcasted_iota(
        jnp.int32, (rows_count, cols_count), 1
    )
    theta = (product % period).astype(jnp.float32) * (2.0 * math.pi / period)
    return (jnp.cos(theta), jnp.sin(theta))


def forward_transform(signal, outer, inner):
    channels = signal.shape[0]
    precise = lax.Precision.HIGHEST
    cos_outer, sin_outer = angle_table(outer, outer, outer)
    blocks = signal.reshape(channels, outer // 2, inner)
    cos_outer = cos_outer[:, : outer // 2]
    sin_outer = sin_outer[:, : outer // 2]
    first_re = jnp.einsum("kn,cnb->ckb", cos_outer, blocks, precision=precise)
    first_im = -jnp.einsum("kn,cnb->ckb", sin_outer, blocks, precision=precise)
    cos_twist, sin_twist = angle_table(outer, inner, outer * inner)
    twist_re = first_re * cos_twist + first_im * sin_twist
    twist_im = first_im * cos_twist - first_re * sin_twist
    cos_inner, sin_inner = angle_table(inner, inner, inner)
    spec_re = jnp.einsum("ckn,nm->ckm", twist_re, cos_inner, precision=precise) + jnp.einsum(
        "ckn,nm->ckm", twist_im, sin_inner, precision=precise
    )
    spec_im = jnp.einsum("ckn,nm->ckm", twist_im, cos_inner, precision=precise) - jnp.einsum(
        "ckn,nm->ckm", twist_re, sin_inner, precision=precise
    )
    return (spec_re, spec_im)


def inverse_transform(spec_re, spec_im, outer, inner):
    channels = spec_re.shape[0]
    precise = lax.Precision.HIGHEST
    cos_inner, sin_inner = angle_table(inner, inner, inner)
    back_re = jnp.einsum("ckm,mn->ckn", spec_re, cos_inner, precision=precise) - jnp.einsum(
        "ckm,mn->ckn", spec_im, sin_inner, precision=precise
    )
    back_im = jnp.einsum("ckm,mn->ckn", spec_re, sin_inner, precision=precise) + jnp.einsum(
        "ckm,mn->ckn", spec_im, cos_inner, precision=precise
    )
    cos_twist, sin_twist = angle_table(outer, inner, outer * inner)
    turned_re = back_re * cos_twist - back_im * sin_twist
    turned_im = back_re * sin_twist + back_im * cos_twist
    cos_outer, sin_outer = angle_table(outer, outer, outer)
    cos_outer = cos_outer[: outer // 2]
    sin_outer = sin_outer[: outer // 2]
    result = jnp.einsum("nk,ckb->cnb", cos_outer, turned_re, precision=precise) - jnp.einsum(
        "nk,ckb->cnb", sin_outer, turned_im, precision=precise
    )
    result = result * (1.0 / (outer * inner))
    return result.reshape(channels, outer // 2 * inner)


def short_conv(cols, earlier, taps):
    extended = jnp.concatenate([earlier, cols], axis=1)
    return (
        taps[0][:, None] * extended[:, 2:]
        + taps[1][:, None] * extended[:, 1:-1]
        + taps[2][:, None] * extended[:, :-2]
    )


def local(tokens, w_query, w_key, w_value, short_taps, filters, skip_gain):
    gathered = lax.all_gather(tokens, "tp", axis=1, tiled=True)
    pieces = (
        lax.all_gather(w_query, "tok", axis=0, tiled=True),
        lax.all_gather(w_key, "tok", axis=0, tiled=True),
        lax.all_gather(w_value, "tok", axis=0, tiled=True),
    )
    query_cols, key_cols, value_cols = tuple(
        (
            lax.dot_general(
                piece, gathered, (((0,), (1,)), ((), ())), preferred_element_type=jnp.float32
            )
            for piece in pieces
        )
    )
    query_prev, key_prev, value_prev = passed_along(
        (query_cols[:, -2:], key_cols[:, -2:], value_cols[:, -2:]), "tok", 1
    )
    query = short_conv(query_cols, query_prev, short_taps[0]).astype(jnp.bfloat16)
    keyed = short_conv(key_cols, key_prev, short_taps[1])
    valued = short_conv(value_cols, value_prev, short_taps[2])
    key_value = (keyed * valued).astype(jnp.bfloat16)
    owned = lax.all_to_all(key_value, "tok", split_axis=0, concat_axis=1, tiled=True)
    signal = owned.astype(jnp.float32)
    length = signal.shape[1]
    outer, inner = split_lengths(length)
    unit = filters / jnp.sqrt(jnp.sum(filters * filters, axis=1, keepdims=True) + 1e-06)
    sig_re, sig_im = forward_transform(signal, outer, inner)
    filt_re, filt_im = forward_transform(unit, outer, inner)
    prod_re = sig_re * filt_re - sig_im * filt_im
    prod_im = sig_re * filt_im + sig_im * filt_re
    convolved = inverse_transform(prod_re, prod_im, outer, inner)
    mixed = (convolved + skip_gain[:, None] * signal).astype(jnp.bfloat16)
    returned = lax.all_to_all(mixed, "tok", split_axis=1, concat_axis=0, tiled=True)
    result = (query.astype(jnp.float32) * returned.astype(jnp.float32)).astype(jnp.bfloat16)
    return result.T


def solution(mesh):
    in_specs = (
        P("tok", "tp"),
        P("tok", "tp"),
        P("tok", "tp"),
        P("tok", "tp"),
        P(None, None, "tp"),
        P(("tp", "tok"), None),
        P(("tp", "tok")),
    )
    out_specs = P("tok", "tp")
    return jax.shard_map(local, mesh=mesh, in_specs=in_specs, out_specs=out_specs, check_vma=False)
```

profile of v0, /device:TPU:0, one launch (start us, length us, event | category | flops | bytes accessed | tf_op | source)
XLA Modules:
  0.0 646.1 jit_solution(3222449162205095284)
XLA Ops:
  9.9 197.8 %all-gather.6.cloned.1.call-done = bf16[4096,4096]{1,0:T(8,128)(2,1)} async-done(((bf16[128,4096]{1,0:T(8,128)(2,1)}), bf16[4096,4096]{1,0:T(8,128)(2,1)}) %all-gather.6.cloned.1.call-update) | async-done | bytes 33554448 | tf_op jit(solution)/shard_map/all_gather | solution.py:91
  207.7 13.7 %fusion.178 = f32[4096,128]{0,1:T(8,128)S(1)} fusion(bf16[128,4096]{1,0:T(8,128)(2,1)S(1)} %copy-done, bf16[4096,4096]{1,0:T(8,128)(2,1)} %all-gather.6.cloned.1.call-done), kind=kOutput, calls=%fused_computation.198 | convolution fusion | flops 4294967296 | bytes 36700160 | tf_op jit(solution)/shard_map/dot_general | solution.py:96
  223.6 180.3 %all-gather.8.cloned.1.call-done = bf16[4096,4096]{1,0:T(8,128)(2,1)} async-done(((bf16[128,4096]{1,0:T(8,128)(2,1)}), bf16[4096,4096]{1,0:T(8,128)(2,1)}) %all-gather.8.cloned.1.call-update) | async-done | bytes 33554448 | tf_op jit(solution)/shard_map/all_gather | solution.py:92
  403.9 13.7 %fusion.179 = f32[4096,128]{0,1:T(8,128)S(1)} fusion(bf16[128,4096]{1,0:T(8,128)(2,1)S(1)} %copy-done, bf16[4096,4096]{1,0:T(8,128)(2,1)} %all-gather.8.cloned.1.call-done), kind=kOutput, calls=%fused_computation.199 | convolution fusion | flops 4294967296 | bytes 36700160 | tf_op jit(solution)/shard_map/dot_general | solution.py:96
  423.3 6.9 %all-to-all-start = ((bf16[32,128,128]{1,2,0:T(8,128)(2,1)}), bf16[32,128,128]{1,2,0:T(8,128)(2,1)S(1)}, u32[]{:S(2)}, u32[]{:S(2)}) async-start(bf16[32,128,128]{1,2,0:T(8,128)(2,1)} %copy_bitcast_fusion), calls=%async_computation | async-start | bytes 2097152 | tf_op jit(solution)/shard_map/all_to_all | solution.py:109
  435.0 9.4 %fusion.64 = f32[128,64,128]{2,0,1:T(8,128)} fusion(f32[128,64,64]{0,2,1:T(8,128)S(1)} %bitcast.120, f32[128,128]{0,1:T(8,128)S(1)} %fusion.108), kind=kOutput, calls=%fused_computation.82 | convolution fusion | flops 805306368 | bytes 6324224 | tf_op jit(solution)/shard_map/kn,cnb->ckb/dot_general | solution.py:41
  444.4 9.4 %fusion.66 = f32[128,64,128]{2,0,1:T(8,128)} fusion(f32[128,64,64]{0,2,1:T(8,128)S(1)} %bitcast.121, f32[128,128]{0,1:T(8,128)S(1)} %fusion.109), kind=kOutput, calls=%fused_computation.84 | convolution fusion | flops 805306368 | bytes 6324224 | tf_op jit(solution)/shard_map/kn,cnb->ckb/dot_general | solution.py:40
  453.8 15.8 %all-to-all-done = bf16[32,128,128]{1,2,0:T(8,128)(2,1)S(1)} async-done(((bf16[32,128,128]{1,2,0:T(8,128)(2,1)}), bf16[32,128,128]{1,2,0:T(8,128)(2,1)S(1)}, u32[]{:S(2)}, u32[]{:S(2)}) %all-to-all-start) | async-done | bytes 1048608 | tf_op jit(solution)/shard_map/all_to_all | solution.py:109
  469.5 5.4 fusion.72
  475.0 8.9 %fusion = (f32[128,128,64]{1,0,2:T(8,128)S(1)}, f32[128,128,64]{1,0,2:T(8,128)S(1)}, f32[128,128,64]{1,0,2:T(8,128)S(1)}, f32[128,128,64]{1,0,2:T(8,128)S(1)}) fusion(f32[128,64,128]{2,0,1:T(8,128)} %fusion.66, f32[128,64,128]{2,0,1:T(8,128)} %fusion.64, f32[128,64]{0,1:T(8,128)S(1)} %get-tuple-element.22, f32[128,64]{0,1:T(8,128)S(1)} %get-tuple-element.23, ...), kind=kOutput, calls=%fused_computation.2 | convolution fusion | flops 819986432 | bytes 30507008 | tf_op jit(solution)/shard_map/kn,cnb->ckb/dot_general | solution.py:40
  483.9 6.4 fusion.14
  490.4 6.6 %fusion.12 = f32[128,128,64]{1,2,0:T(8,128)S(1)} fusion(f32[128,128,64]{1,0,2:T(8,128)S(1)} %get-tuple-element.8), kind=kOutput, calls=%fused_computation.24 | convolution fusion | flops 805363712 | bytes 8388608 | tf_op jit(solution)/shard_map/ckn,nm->ckm/dot_general | solution.py:49
  497.0 6.7 %fusion.22 = f32[128,128,64]{1,2,0:T(8,128)S(1)} fusion(f32[128,128,64]{1,0,2:T(8,128)S(1)} %get-tuple-element.20), kind=kOutput, calls=%fused_computation.34 | convolution fusion | flops 805363712 | bytes 8388608 | tf_op jit(solution)/shard_map/ckn,nm->ckm/dot_general | solution.py:46
  503.7 9.3 %fusion.20 = f32[128,128,64]{1,2,0:T(8,128)} fusion(f32[128,128,64]{1,0,2:T(8,128)S(1)} %get-tuple-element.20), kind=kOutput, calls=%fused_computation.32 | convolution fusion | flops 805363712 | bytes 8388608 | tf_op jit(solution)/shard_map/ckn,nm->ckm/dot_general | solution.py:49
  512.9 6.8 %fusion.34 = f32[128,128,64]{1,2,0:T(8,128)S(1)} fusion(f32[128,128,64]{1,2,0:T(8,128)S(1)} %fusion.14, f32[128,128,64]{1,0,2:T(8,128)S(1)} %get-tuple-element.7), kind=kOutput, calls=%fused_computation.48 | convolution fusion | flops 806412288 | bytes 12582912 | tf_op jit(solution)/shard_map/ckn,nm->ckm/dot_general | solution.py:46
  519.7 7.2 %fusion.37 = f32[128,128,64]{1,2,0:T(8,128)S(1)} fusion(f32[128,128,64]{1,2,0:T(8,128)S(1)} %fusion.12, f32[128,128,64]{1,0,2:T(8,128)S(1)} %get-tuple-element.7), kind=kOutput, calls=%fused_computation.49 | convolution fusion | flops 806412288 | bytes 12582912 | tf_op jit(solution)/shard_map/ckn,nm->ckm/dot_general | solution.py:49
  526.9 9.2 %fusion.28 = f32[128,128,64]{1,2,0:T(8,128)} fusion(f32[128,128,64]{1,2,0:T(8,128)S(1)} %fusion.22, f32[128,128,64]{1,0,2:T(8,128)S(1)} %get-tuple-element.21), kind=kOutput, calls=%fused_computation.46 | convolution fusion | flops 806412288 | bytes 12582912 | tf_op jit(solution)/shard_map/ckn,nm->ckm/dot_general | solution.py:46
  536.2 11.8 %multiply_subtract_fusion = (f32[128,128,64]{1,2,0:T(8,128)S(1)}, f32[128,128,64]{1,2,0:T(8,128)S(1)}) fusion(f32[128,128,64]{1,2,0:T(8,128)S(1)} %fusion.37, f32[128,128,64]{1,2,0:T(8,128)} %fusion.28, f32[128,128,64]{1,2,0:T(8,128)S(1)} %fusion.34, f32[128,128,64]{1,2,0:T(8,128)} %fusion.20, f32[128,128,64]{1,0,2:T(8,128)S(1)} %get-tuple-element.21), kind=kOutput, calls=%fused_computation.23 | convolution fusion | flops 812703744 | bytes 29360128 | tf_op jit(solution)/shard_map/ckn,nm->ckm/dot_general | solution.py:49
  556.7 4.5 fusion.88
  565.7 18.1 %fusion.4 = f32[128,64,64]{0,2,1:T(8,128)S(1)} fusion(f32[128,64]{0,1:T(8,128)S(1)} %get-tuple-element.22, f32[128,64]{0,1:T(8,128)S(1)} %get-tuple-element.23, f32[128,128,64]{1,2,0:T(8,128)S(1)} %fusion.90, f32[128,128,64]{1,2,0:T(8,128)S(1)} %fusion.98, f32[128,128,64]{1,2,0:T(8,128)S(1)} %fusion.96, f32[128,128,64]{1,2,0:T(8,128)S(1)} %fusion.88, ...), kind=kOutput, calls=%fused_computation.14 | convolution fusion | flops 810549248 | bytes 19005440 | tf_op jit(solution)/shard_map/nk,ckb->cnb/dot_general | solution.py:71
  583.8 18.1 %multiply_bitcast_fusion = f32[128,64,64]{0,1,2:T(8,128)S(1)} fusion(f32[128,64,64]{0,2,1:T(8,128)S(1)} %fusion.4, f32[128,64]{0,1:T(8,128)S(1)} %get-tuple-element.22, f32[128,64]{0,1:T(8,128)S(1)} %get-tuple-element.23, f32[128,128,64]{1,2,0:T(8,128)S(1)} %fusion.90, f32[128,128,64]{1,2,0:T(8,128)S(1)} %fusion.98, f32[128,128,64]{1,2,0:T(8,128)S(1)} %fusion.96, ...), kind=kOutput, calls=%fused_computation.76 | convolution fusion | flops 811597824 | bytes 21102592 | tf_op jit(solution)/shard_map/nk,ckb->cnb/dot_general | solution.py:71
  604.5 5.7 all-to-all-start.1
  613.4 12.9 %fusion.177 = f32[4096,128]{0,1:T(8,128)S(1)} fusion(bf16[128,4096]{1,0:T(8,128)(2,1)S(1)} %copy-done, bf16[4096,4096]{1,0:T(8,128)(2,1)} %all-gather.4.cloned.1.call-done), kind=kOutput, calls=%fused_computation.197 | convolution fusion | flops 4294967296 | bytes 36700160 | tf_op jit(solution)/shard_map/dot_general | solution.py:96
  629.3 7.0 %all-to-all-done.1 = bf16[128,32,128]{0,2,1:T(8,128)(2,1)} async-done(((bf16[128,32,128]{0,2,1:T(8,128)(2,1)}), bf16[128,32,128]{0,2,1:T(8,128)(2,1)}, u32[]{:S(2)}, u32[]{:S(2)}) %all-to-all-start.1) | async-done | bytes 1048608 | tf_op jit(solution)/shard_map/all_to_all | solution.py:120
  (45 shorter events, 40.9 us)
Async XLA Ops:
  6.5 201.2 %copy-start = (bf16[128,4096]{1,0:T(8,128)(2,1)S(1)}, bf16[128,4096]{1,0:T(8,128)(2,1)}, u32[]{:S(2)}) copy-start(bf16[128,4096]{1,0:T(8,128)(2,1)} %param.7) | copy-start | bytes 3145732
  6.5 2.5 copy-start.3
  6.5 3.3 copy-start.4
  6.5 201.2 %all-gather.6.cloned.1.call-start = ((), (), s32[]{:S(2)}) async-start(), calls=%async_computation.3 | async-start | bytes 34603008 | tf_op jit(solution)/shard_map/all_gather | solution.py:91
  7.3 396.6 %all-gather.8.cloned.1.call-start = ((), (), s32[]{:S(2)}) async-start(), calls=%async_computation.4 | async-start | bytes 34603008 | tf_op jit(solution)/shard_map/all_gather | solution.py:92
  8.0 605.4 %all-gather.4.cloned.1.call-start = ((), (), s32[]{:S(2)}) async-start(), calls=%async_computation.2 | async-start | bytes 34603008 | tf_op jit(solution)/shard_map/all_gather | solution.py:90
  221.4 198.6 %collective-permute-start.1 = (f32[4096,2]{0,1:T(2,128)S(1)}, f32[4096,2]{0,1:T(2,128)S(1)}, u32[]{:S(2)}, u32[]{:S(2)}) collective-permute-start(f32[4096,2]{0,1:T(2,128)S(1)} %slice.118), channel_id=1, source_target_pairs={{0,1},{1,2},{2,3},{3,4},{4,5},{5,6},{6,7},{7,8},{8,9},{9,10},{10,1... | collective-permute-start | bytes 98312 | tf_op jit(solution)/shard_map/ppermute | solution.py:12
  417.6 3.0 collective-permute-start.2
  423.3 9.9 %copy-start.6 = (f32[128]{0:T(128)S(1)}, f32[128]{0:T(128)}, u32[]{:S(2)}) copy-start(f32[128]{0:T(128)} %multiply_reduce_fusion) | copy-start | bytes 1540
  423.3 46.3 %all-to-all-start = ((bf16[32,128,128]{1,2,0:T(8,128)(2,1)}), bf16[32,128,128]{1,2,0:T(8,128)(2,1)S(1)}, u32[]{:S(2)}, u32[]{:S(2)}) async-start(bf16[32,128,128]{1,2,0:T(8,128)(2,1)} %copy_bitcast_fusion), calls=%async_computation | async-start | bytes 2097152 | tf_op jit(solution)/shard_map/all_to_all | solution.py:109
  469.5 14.4 %copy-start.1 = (bf16[32,128,128]{1,2,0:T(8,128)(2,1)}, bf16[32,128,128]{1,2,0:T(8,128)(2,1)S(1)}, u32[]{:S(2)}) copy-start(bf16[32,128,128]{1,2,0:T(8,128)(2,1)S(1)} %all-to-all-done) | copy-start | bytes 3145732
  601.9 1.3 copy-start.2
  601.9 1.2 copy-start.5
  604.5 31.9 %all-to-all-start.1 = ((bf16[128,32,128]{0,2,1:T(8,128)(2,1)}), bf16[128,32,128]{0,2,1:T(8,128)(2,1)}, u32[]{:S(2)}, u32[]{:S(2)}) async-start(bf16[128,32,128]{0,2,1:T(8,128)(2,1)} %fusion.59), calls=%async_computation.1 | async-start | bytes 2097152 | tf_op jit(solution)/shard_map/all_to_all | solution.py:120
  626.3 3.0 collective-permute-start
Sparse Core Ops, SparseCore 0:
  10.2 197.4 all-gather.5
  210.6 193.2 all-gather.7
  406.8 206.5 all-gather.3
where the time goes:
time: 652 us; the launch traced here: 646 us
  waiting for transfers between devices  408 us (63%)
  matrix products  191 us (29%)
  starting transfers between devices  19.1 us (3%)
  between operations  13.6 us (2%)
  other arithmetic  10.2 us (2%)
    all_gather x1, waiting for transfers between devices, local(): lax.all_gather(w_key, 'tok', axis=0, tiled=True)  198 us
    all_gather x1, waiting for transfers between devices, local(): lax.all_gather(w_value, 'tok', axis=0, tiled=True)  180 us
    dot_general x3, matrix products, local(): lax.dot_general(piece, gathered, (((0,), (1,)), ((), ())), preferred_elem...  40.2 us
    dot_general x2, matrix products, forward_transform(): jnp.einsum('ckn,nm->ckm', twist_re, sin_inner, precision=precise)  19.1 us
    dot_general x2, matrix products, forward_transform(): first_re = jnp.einsum('kn,cnb->ckb', cos_outer, blocks, precision=precise)  18.3 us
    dot_general x1, matrix products, inverse_transform(): jnp.einsum('nk,ckb->cnb', cos_outer, turned_re, precision=precise)  18.1 us
    dot_general x1, matrix products, inverse_transform(): jnp.einsum('nk,ckb->cnb', sin_outer, turned_im, precision=precise)  18.1 us
    dot_general x2, matrix products, forward_transform(): jnp.einsum('ckn,nm->ckm', twist_re, cos_inner, precision=precise)  16 us
  transfers between devices with their start and end apart: 8, of which 7 were waited for; matrix products, arithmetic and copies ran while one was open for 31% of the time, Pallas kernels for 0%

commit v1 on v0

--- a/solution.py
+++ b/solution.py
@@ -84,7 +84,7 @@
     )
 
 
-def local(tokens, w_query, w_key, w_value, short_taps, filters, skip_gain):
+def local_by_tokens(tokens, w_query, w_key, w_value, short_taps, filters, skip_gain):
     gathered = lax.all_gather(tokens, "tp", axis=1, tiled=True)
     pieces = (
         lax.all_gather(w_query, "tok", axis=0, tiled=True),
@@ -122,6 +122,101 @@
     return result.T
 
 
+def unit_circle(phase, period):
+    theta = (phase % period).astype(jnp.float32) * (2.0 * math.pi / period)
+    return (jnp.cos(theta), jnp.sin(theta))
+
+
+def quarter_tables(outer, inner):
+    length = outer * inner
+    iota = lax.broadcasted_iota
+    k1 = iota(jnp.int32, (outer, outer), 0)
+    n1 = iota(jnp.int32, (outer, outer), 1)
+    cos1, sin1 = unit_circle((4 * k1 + 1) * n1, 4 * outer)
+    outer_fwd = jnp.stack([cos1, -sin1], axis=1).reshape(2 * outer, outer)
+    outer_inv = jnp.stack([cos1, -sin1], axis=1).reshape(2 * outer, outer).T
+    k1 = iota(jnp.int32, (outer, inner), 0)
+    n2 = iota(jnp.int32, (outer, inner), 1)
+    twist = unit_circle((4 * k1 + 1) * n2, 4 * length)
+    k2 = iota(jnp.int32, (inner, inner), 0)
+    n2 = iota(jnp.int32, (inner, inner), 1)
+    cos2, sin2 = unit_circle(k2 * n2, inner)
+    inner_fwd = jnp.concatenate(
+        [jnp.concatenate([cos2, sin2], 1), jnp.concatenate([-sin2, cos2], 1)], 0
+    )
+    inner_inv = jnp.concatenate(
+        [jnp.concatenate([cos2, -sin2], 1), jnp.concatenate([sin2, cos2], 1)], 0
+    )
+    return outer_fwd, outer_inv, twist, inner_fwd, inner_inv * (1.0 / length)
+
+
+def mul16(spec, a, b):
+    return jnp.einsum(
+        spec, a.astype(jnp.bfloat16), b.astype(jnp.bfloat16), preferred_element_type=jnp.float32
+    )
+
+
+def quarter_forward(signal, tables, outer, inner):
+    outer_fwd, _, (cos_t, sin_t), inner_fwd, _ = tables
+    channels = signal.shape[1]
+    first = mul16("kn,nc->kc", outer_fwd, signal.reshape(outer, inner * channels))
+    first = first.reshape(outer, 2, inner, channels)
+    re, im = first[:, 0], first[:, 1]
+    cos_t, sin_t = cos_t[:, :, None], sin_t[:, :, None]
+    turned = jnp.concatenate([re * cos_t + im * sin_t, im * cos_t - re * sin_t], axis=1)
+    return mul16("mn,knc->kmc", inner_fwd, turned).reshape(outer, 2, inner, channels)
+
+
+def quarter_inverse(spec_re, spec_im, tables, outer, inner):
+    _, outer_inv, (cos_t, sin_t), _, inner_inv = tables
+    channels = spec_re.shape[2]
+    spectrum = jnp.concatenate([spec_re, spec_im], axis=1)
+    back = mul16("mn,knc->kmc", inner_inv, spectrum).reshape(outer, 2, inner, channels)
+    re, im = back[:, 0], back[:, 1]
+    cos_t, sin_t = cos_t[:, :, None], sin_t[:, :, None]
+    turned = jnp.stack([re * cos_t - im * sin_t, re * sin_t + im * cos_t], axis=1)
+    result = mul16("nk,kc->nc", outer_inv, turned.reshape(2 * outer, inner * channels))
+    return result.reshape(outer * inner, channels)
+
+
+def balanced(length):
+    inner = max(d for d in range(1, int(math.isqrt(length)) + 1) if length % d == 0)
+    return (length // inner, inner)
+
+
+def long_conv(signal, filters_t, tables, outer, inner):
+    unit = filters_t * lax.rsqrt(jnp.sum(filters_t * filters_t, axis=0, keepdims=True) + 1e-06)
+    filt = quarter_forward(unit, tables, outer, inner)
+    sig = quarter_forward(signal, tables, outer, inner)
+    sig_re, sig_im, filt_re, filt_im = sig[:, 0], sig[:, 1], filt[:, 0], filt[:, 1]
+    prod_re = sig_re * filt_re - sig_im * filt_im
+    prod_im = sig_re * filt_im + sig_im * filt_re
+    return quarter_inverse(prod_re, prod_im, tables, outer, inner)
+
+
+def short_rows(raw, taps):
+    padded = jnp.pad(raw, ((2, 0), (0, 0)))
+    return taps[0] * raw + taps[1] * padded[1:-1] + taps[2] * padded[:-2]
+
+
+def local_by_channels(tokens, w_query, w_key, w_value, short_taps, filters, skip_gain):
+    owned = filters.shape[0]
+    start = lax.axis_index("tok") * owned
+    gathered = lax.all_gather(tokens, "tok", axis=0, tiled=True)
+    weights = jnp.stack([w_query, w_key, w_value])
+    weights = lax.all_to_all(weights, "tok", split_axis=2, concat_axis=1, tiled=True)
+    raw = jnp.einsum("tk,pkc->ptc", gathered, weights, preferred_element_type=jnp.float32)
+    taps = lax.dynamic_slice_in_dim(short_taps, start, owned, axis=2)
+    query = short_rows(raw[0], taps[0]).astype(jnp.bfloat16)
+    key_value = (short_rows(raw[1], taps[1]) * short_rows(raw[2], taps[2])).astype(jnp.bfloat16)
+    outer, inner = balanced(filters.shape[1])
+    tables = quarter_tables(outer, inner)
+    convolved = long_conv(key_value, filters.T, tables, outer, inner)
+    mixed = (convolved + skip_gain[None, :] * key_value.astype(jnp.float32)).astype(jnp.bfloat16)
+    result = (query.astype(jnp.float32) * mixed.astype(jnp.float32)).astype(jnp.bfloat16)
+    return lax.all_to_all(result, "tok", split_axis=0, concat_axis=1, tiled=True)
+
+
 def solution(mesh):
     in_specs = (
         P("tok", "tp"),
@@ -133,4 +228,5 @@
         P(("tp", "tok")),
     )
     out_specs = P("tok", "tp")
+    local = local_by_channels if mesh.shape["tp"] == 1 else local_by_tokens
     return jax.shard_map(local, mesh=mesh, in_specs=in_specs, out_specs=out_specs, check_vma=False)

time: 652 us -> 367 us (0.56)
  waiting for transfers between devices: 408 us -> 243 us
  matrix products: 191 us -> 30.5 us
  blocking collectives: 0 us -> 28.8 us
  local copies, waits for them, and re-layouts: 4.31 us -> 28.6 us
  starting transfers between devices: 19.1 us -> 7.43 us
    all_gather x3 -> x1, waiting for transfers between devices: 381 us -> 87.7 us  [local_by_channels(): gathered = lax.all_gather(tokens, 'tok', axis=0, tiled=True)]
    dot_general x21 -> x7, matrix products: 191 us -> 30.5 us  [the longest x1 21.7 us: local_by_channels(): jnp.einsum('tk,pkc->ptc', gathered, weights, preferred_element_type=jnp.f...]
    all_to_all x2 -> x1, waiting for transfers between devices: 22.8 us -> 154 us  [local_by_channels(): lax.all_to_all(weights, 'tok', split_axis=2, concat_axis=1, tiled=True)]
    all_to_all x0 -> x1, blocking collectives: none -> 28.8 us  [local_by_channels(): lax.all_to_all(result, 'tok', split_axis=0, concat_axis=1, tiled=True)]
    all_to_all x0 -> x3, local copies, waits for them, and re-layouts: none -> 10.7 us  [the longest x2 9.36 us: local_by_channels(): lax.all_to_all(weights, 'tok', split_axis=2, concat_axis=1, tiled=True)]
  transfers between devices with their start and end apart: 8 -> 2, of which waited for: 7 -> 2; matrix products, arithmetic and copies ran while one was open for 31% -> 5% of each run, Pallas kernels for 0% -> 0%
where the time goes in v1:
time: 367 us
  waiting for transfers between devices  243 us (66%)
  matrix products  30.5 us (8%)
  blocking collectives  28.8 us (8%)
  local copies, waits for them, and re-layouts  28.6 us (8%)
  other arithmetic  15.1 us (4%)
  between operations  13.6 us (4%)
  starting transfers between devices  7.43 us (2%)
    all_to_all x1, waiting for transfers between devices, local_by_channels(): lax.all_to_all(weights, 'tok', split_axis=2, concat_axis=1, tiled=True)  154 us
    all_gather x1, waiting for transfers between devices, local_by_channels(): gathered = lax.all_gather(tokens, 'tok', axis=0, tiled=True)  87.7 us
    all_to_all x1, blocking collectives, local_by_channels(): lax.all_to_all(result, 'tok', split_axis=0, concat_axis=1, tiled=True)  28.8 us
    dot_general x1, matrix products, local_by_channels(): jnp.einsum('tk,pkc->ptc', gathered, weights, preferred_element_type=jnp.f...  21.7 us
    all_to_all x2, local copies, waits for them, and re-layouts, local_by_channels(): lax.all_to_all(weights, 'tok', split_axis=2, concat_axis=1, tiled=True)  9.36 us
    dot_general x6, matrix products, mul16(): jnp.einsum(spec, a.astype(jnp.bfloat16), b.astype(jnp.bfloat16), preferre...  8.84 us
    all_to_all x1, starting transfers between devices, local_by_channels(): lax.all_to_all(weights, 'tok', split_axis=2, concat_axis=1, tiled=True)  7.43 us
  transfers between devices with their start and end apart: 2, of which 2 were waited for; matrix products, arithmetic and copies ran while one was open for 5% of the time, Pallas kernels for 0%

profile of v1, /device:TPU:0, one launch (start us, length us, event | category | flops | bytes accessed | tf_op | source)
XLA Modules:
  0.0 367.0 jit_solution(2006358779258068897)
XLA Ops:
  7.3 2.2 pad_maximum_fusion
  9.5 4.7 %copy.54 = bf16[3,128,4096]{1,0,2:T(4,128)(2,1)} copy(bf16[3,128,4096]{2,1,0:T(8,128)(2,1)S(1)} %pad_maximum_fusion) | data formatting | bytes 6291456 | tf_op jit(solution)/shard_map/stack | solution.py:206
  14.2 7.4 %all-to-all-start = ((bf16[3,128,4096]{1,0,2:T(4,128)(2,1)}), bf16[3,128,4096]{1,0,2:T(4,128)(2,1)}, u32[]{:S(2)}, u32[]{:S(2)}) async-start(bf16[3,128,4096]{1,0,2:T(4,128)(2,1)} %copy.54), calls=%async_computation | async-start | bytes 8388608 | tf_op jit(solution)/shard_map/all_to_all | solution.py:207
  23.9 0.9 fusion.58
  25.5 2.6 fusion.19
  28.1 154.5 %all-to-all-done = bf16[3,128,4096]{1,0,2:T(4,128)(2,1)} async-done(((bf16[3,128,4096]{1,0,2:T(4,128)(2,1)}), bf16[3,128,4096]{1,0,2:T(4,128)(2,1)}, u32[]{:S(2)}, u32[]{:S(2)}) %all-to-all-start) | async-done | bytes 3145760 | tf_op jit(solution)/shard_map/all_to_all | solution.py:207
  182.6 6.0 %copy.99 = bf16[3,128,32,128]{1,2,3,0:T(8,128)(2,1)S(1)} copy(bf16[3,128,32,128]{1,0,3,2:T(4,128)(2,1)} %bitcast.4) | data formatting | bytes 6291456 | tf_op jit(solution)/shard_map/all_to_all | solution.py:207
  188.6 3.3 all_to_all.30
  192.0 87.7 %all-gather.2.cloned.1.call-done = bf16[4096,4096]{1,0:T(8,128)(2,1)} async-done(((bf16[128,4096]{1,0:T(8,128)(2,1)}), bf16[4096,4096]{1,0:T(8,128)(2,1)}) %all-gather.2.cloned.1.call-update) | async-done | bytes 33554448 | tf_op jit(solution)/shard_map/all_gather | solution.py:205
  279.7 21.7 %fusion.2 = f32[3,4096,128]{1,2,0:T(8,128)} fusion(bf16[3,4096,128]{1,2,0:T(8,128)(2,1)} %all_to_all.30, bf16[4096,4096]{1,0:T(8,128)(2,1)} %all-gather.2.cloned.1.call-done), kind=kOutput, calls=%fused_computation.2 | convolution fusion | flops 12884901888 | bytes 42991616 | tf_op jit(solution)/shard_map/tk,pkc->ptc/dot_general | solution.py:208
  301.4 4.7 %slice_bitcast_fusion.10 = (f32[4096,128]{0,1:T(8,128)}, f32[4096,128]{0,1:T(8,128)S(1)}, f32[4096,128]{0,1:T(8,128)S(1)}) fusion(f32[3,4096,128]{1,2,0:T(8,128)} %fusion.2), kind=kLoop, calls=%fused_computation.18 | loop fusion | bytes 12582912 | tf_op jit(solution)/shard_map/squeeze | solution.py:210
  306.1 2.6 multiply_convert_fusion.2
  310.7 1.5 copy-done
  312.2 1.8 add_convert_fusion.4
  314.3 1.6 fusion.14
  316.0 1.6 fusion.12
  317.6 1.1 fusion.17
  319.4 1.4 subtract_convert_fusion
  321.1 1.5 fusion.5
  322.5 1.5 reshape.203
  324.0 1.9 copy.69
  326.0 4.1 %copy_bitcast_fusion.1 = bf16[32,128,128]{1,2,0:T(8,128)(2,1)S(1)} fusion(f32[4096,128]{0,1:T(8,128)S(1)} %copy.69, bf16[4096,128]{0,1:T(8,128)(2,1)S(1)} %multiply_convert_fusion.2, f32[128]{0:T(128)S(1)} %copy-done.2, f32[128]{0:T(128)S(1)} %get-tuple-element.22, f32[4096,128]{0,1:T(8,128)} %get-tuple-element.7, f32[128]{0:T(128)S(1)} %get-tuple-element.23, ...), kind=kLoop, calls=%fused_computation.47 | loop fusion | flops 7340032 | bytes 6293504 | tf_op jit(solution)/shard_map/all_to_all | solution.py:217
  330.0 28.8 %all_to_all.37 = bf16[32,128,128]{1,2,0:T(8,128)(2,1)S(1)} all-to-all(bf16[32,128,128]{1,2,0:T(8,128)(2,1)S(1)} %copy_bitcast_fusion.1), channel_id=1, replica_groups=mesh['tok'=32,'tp'=1] {'tok'}, dimensions={0} | all-to-all | bytes 2097152 | tf_op jit(solution)/shard_map/all_to_all | solution.py:217
  358.9 1.3 copy.71
  (29 shorter events, 6.9 us)
Async XLA Ops:
  6.5 273.2 %all-gather.2.cloned.1.call-start = ((), (), s32[]{:S(2)}) async-start(), calls=%async_computation.2 | async-start | bytes 34603008 | tf_op jit(solution)/shard_map/all_gather | solution.py:205
  14.2 7.4 %copy-start.1 = (f32[128,4096]{1,0:T(8,128)S(1)}, f32[128,4096]{1,0:T(8,128)}, u32[]{:S(2)}) copy-start(f32[128,4096]{1,0:T(8,128)} %param.12) | copy-start | bytes 6291460
  14.2 168.4 %all-to-all-start = ((bf16[3,128,4096]{1,0,2:T(4,128)(2,1)}), bf16[3,128,4096]{1,0,2:T(4,128)(2,1)}, u32[]{:S(2)}, u32[]{:S(2)}) async-start(bf16[3,128,4096]{1,0,2:T(4,128)(2,1)} %copy.54), calls=%async_computation | async-start | bytes 8388608 | tf_op jit(solution)/shard_map/all_to_all | solution.py:207
  310.0 2.2 copy-start
  324.0 1.9 copy-start.2
Sparse Core Ops, SparseCore 0:
  10.2 269.4 all-gather.1

commit v2 on v1

--- a/solution.py
+++ b/solution.py
@@ -1,8 +1,11 @@
+import functools
 import math
 
 import jax
 import jax.numpy as jnp
 from jax import lax
+from jax.experimental import pallas as pl
+from jax.experimental.pallas import tpu as pltpu
 from jax.sharding import PartitionSpec as P
 
 
@@ -194,6 +197,177 @@
     return quarter_inverse(prod_re, prod_im, tables, outer, inner)
 
 
+def exchange_kernel(
+    count, tok_ref, w_ref, all_tok, all_w, send_sem, recv_sem, w_send, w_recv, local_sem
+):
+    me = lax.axis_index("tok")
+    depth = count // 8
+    core, x, y, z = (lax.rem(me, 2), lax.rem(me // 2, 2), lax.rem(me // 4, 2), me // 8)
+    step_core, step_x, step_y = (1 - 2 * core, 2 - 4 * x, 4 - 8 * y)
+    rows = tok_ref.shape[0] // 2
+
+    barrier = pltpu.get_barrier_semaphore()
+
+    @pl.loop(1, count)
+    def _(j):
+        pl.semaphore_signal(
+            barrier,
+            inc=1,
+            device_id={"tok": lax.rem(me + j, count)},
+            device_id_type=pl.DeviceIdType.MESH,
+        )
+
+    pl.semaphore_wait(barrier, count - 1)
+
+    own_tok = pltpu.make_async_copy(tok_ref, all_tok.at[me], local_sem.at[0])
+    own_w = pltpu.make_async_copy(w_ref.at[me], all_w.at[me], local_sem.at[1])
+    own_tok.start()
+    own_w.start()
+
+    def tok_copy(half, block, dest, slot, own=False):
+        part = pl.ds(half * rows, rows)
+        return pltpu.make_async_remote_copy(
+            src_ref=tok_ref.at[part] if own else all_tok.at[block, part],
+            dst_ref=all_tok.at[block, part],
+            send_sem=send_sem.at[half, block // 2, slot],
+            recv_sem=recv_sem.at[half, block],
+            device_id={"tok": dest},
+            device_id_type=pl.DeviceIdType.MESH,
+        )
+
+    sent = []
+
+    def put(cond, half, block, dest, slot, own=False):
+        sent.append((cond, half, block, dest, slot))
+
+        def go():
+            tok_copy(half, block, dest, slot, own).start()
+
+        go() if cond is None else pl.when(cond)(go)
+
+    def arrived(cond, half, block):
+        def go():
+            tok_copy(half, block, me, 0).wait_recv()
+
+        go() if cond is None else pl.when(cond)(go)
+
+    turns = ((step_x, step_y), (step_y, step_x))
+    for half in range(2):
+        first, second = turns[half]
+        put(z + 1 < depth, half, me, me + 8, 0, own=True)
+        put(z > 0, half, me, me - 8, 1, own=True)
+        put(None, half, me, me + first, 2, own=True)
+        put(None, half, me, me + second, 3, own=True)
+        put(None, half, me, me + step_core, 4, own=True)
+
+    def w_copy(j):
+        dest = lax.rem(me + j, count)
+        return pltpu.make_async_remote_copy(
+            src_ref=w_ref.at[dest],
+            dst_ref=all_w.at[me],
+            send_sem=w_send.at[j],
+            recv_sem=w_recv.at[j],
+            device_id={"tok": dest},
+            device_id_type=pl.DeviceIdType.MESH,
+        )
+
+    pl.loop(1, count)(lambda j: w_copy(j).start())
+
+    def both_ways(distance):
+        yield (z >= distance, -8 * distance)
+        if distance:
+            yield (z + distance < depth, 8 * distance)
+
+    def from_first(distance):
+        for half in range(2):
+            first, second = turns[half]
+            for cond, shift in both_ways(distance):
+                block = me + first + shift
+                arrived(cond, half, block)
+                put(cond, half, block, me + second, 3)
+                put(cond, half, block, me + step_core, 4)
+
+    for distance in range(1, depth):
+        for half in range(2):
+            first, second = turns[half]
+            for cond, shift in both_ways(distance):
+                block = me + shift
+                arrived(cond, half, block)
+                if shift < 0:
+                    put(jnp.logical_and(cond, z + 1 < depth), half, block, me + 8, 0)
+                else:
+                    put(jnp.logical_and(cond, z > 0), half, block, me - 8, 1)
+                put(cond, half, block, me + first, 2)
+                put(cond, half, block, me + second, 3)
+                put(cond, half, block, me + step_core, 4)
+        from_first(distance - 1)
+    from_first(depth - 1)
+    for distance in range(depth):
+        for half in range(2):
+            first, second = turns[half]
+            for cond, shift in both_ways(distance):
+                for base in (second, first + second):
+                    block = me + base + shift
+                    arrived(cond, half, block)
+                    put(cond, half, block, me + step_core, 4)
+
+    @pl.loop(0, count // 2)
+    def _(pair):
+        for half in range(2):
+            tok_copy(half, 2 * pair + 1 - core, me, 0).wait_recv()
+
+    for cond, half, block, dest, slot in sent:
+
+        def done(half=half, block=block, dest=dest, slot=slot):
+            tok_copy(half, block, dest, slot).wait_send()
+
+        done() if cond is None else pl.when(cond)(done)
+
+    @pl.loop(1, count)
+    def _(j):
+        w_copy(j).wait_recv()
+        w_copy(j).wait_send()
+
+    own_tok.wait()
+    own_w.wait()
+
+
+def exchanged(tokens, weights):
+    count = lax.axis_size("tok")
+    anywhere = pl.BlockSpec(memory_space=pl.ANY)
+    return pl.pallas_call(
+        functools.partial(exchange_kernel, count),
+        out_shape=(
+            jax.ShapeDtypeStruct((count,) + tokens.shape, tokens.dtype),
+            jax.ShapeDtypeStruct(weights.shape, weights.dtype),
+        ),
+        in_specs=[anywhere, anywhere],
+        out_specs=(anywhere, anywhere),
+        scratch_shapes=[
+            pltpu.SemaphoreType.DMA((2, count // 2, 5)),
+            pltpu.SemaphoreType.DMA((2, count)),
+            pltpu.SemaphoreType.DMA((count,)),
+            pltpu.SemaphoreType.DMA((count,)),
+            pltpu.SemaphoreType.DMA((2,)),
+        ],
+        compiler_params=pltpu.CompilerParams(collective_id=0, has_side_effects=True),
+    )(tokens, weights)
+
+
+def gathered_and_columns(tokens, weights):
+    count = lax.axis_size("tok")
+    kinds, depth, channels = weights.shape
+    blocks = weights.reshape(kinds, depth, count, channels // count)
+    blocks = blocks.transpose(2, 1, 0, 3).reshape(count, depth, kinds * channels // count)
+    if count % 8 == 0 and tokens.shape[0] % 32 == 0:
+        all_tokens, columns = exchanged(tokens, blocks)
+        all_tokens = all_tokens.reshape(count * tokens.shape[0], tokens.shape[1])
+    else:
+        all_tokens = lax.all_gather(tokens, "tok", axis=0, tiled=True)
+        columns = lax.all_to_all(blocks, "tok", split_axis=0, concat_axis=0, tiled=True)
+    return all_tokens, columns.reshape(count * depth, kinds * channels // count)
+
+
 def short_rows(raw, taps):
     padded = jnp.pad(raw, ((2, 0), (0, 0)))
     return taps[0] * raw + taps[1] * padded[1:-1] + taps[2] * padded[:-2]
@@ -202,10 +376,9 @@
 def local_by_channels(tokens, w_query, w_key, w_value, short_taps, filters, skip_gain):
     owned = filters.shape[0]
     start = lax.axis_index("tok") * owned
-    gathered = lax.all_gather(tokens, "tok", axis=0, tiled=True)
-    weights = jnp.stack([w_query, w_key, w_value])
-    weights = lax.all_to_all(weights, "tok", split_axis=2, concat_axis=1, tiled=True)
-    raw = jnp.einsum("tk,pkc->ptc", gathered, weights, preferred_element_type=jnp.float32)
+    gathered, columns = gathered_and_columns(tokens, jnp.stack([w_query, w_key, w_value]))
+    raw = jnp.dot(gathered, columns, preferred_element_type=jnp.float32)
+    raw = [raw[:, kind * owned : (kind + 1) * owned] for kind in range(3)]
     taps = lax.dynamic_slice_in_dim(short_taps, start, owned, axis=2)
     query = short_rows(raw[0], taps[0]).astype(jnp.bfloat16)
     key_value = (short_rows(raw[1], taps[1]) * short_rows(raw[2], taps[2])).astype(jnp.bfloat16)

time: 367 us -> 286 us (0.78)
  waiting for transfers between devices: 243 us -> 0 us
  Pallas kernels: 0 us -> 185 us
  between operations: 13.6 us -> 0.19 us
  local copies, waits for them, and re-layouts: 28.6 us -> 19 us
  starting transfers between devices: 7.43 us -> 0 us
    pallas_call x0 -> x1, Pallas kernels: none -> 185 us  [exchanged(): pl.pallas_call(functools.partial(exchange_kernel, count), out_shape=(jax....]
    all_to_all x1 -> x0, waiting for transfers between devices: 154 us -> none  [local_by_channels(): lax.all_to_all(weights, 'tok', split_axis=2, concat_axis=1, tiled=True)]
    all_gather x1 -> x0, waiting for transfers between devices: 87.7 us -> none  [local_by_channels(): gathered = lax.all_gather(tokens, 'tok', axis=0, tiled=True)]
    all_to_all x2 -> x0, local copies, waits for them, and re-layouts: 9.36 us -> none  [local_by_channels(): lax.all_to_all(weights, 'tok', split_axis=2, concat_axis=1, tiled=True)]
    all_to_all x1 -> x0, starting transfers between devices: 7.43 us -> none  [local_by_channels(): lax.all_to_all(weights, 'tok', split_axis=2, concat_axis=1, tiled=True)]
    unnamed x6 -> x13, local copies, waits for them, and re-layouts: 1.5 us -> 6.47 us
    another operation x1 -> x0, local copies, waits for them, and re-layouts: 4.72 us -> none  [local_by_channels(): weights = jnp.stack([w_query, w_key, w_value])]
    squeeze x1 -> x0, local copies, waits for them, and re-layouts: 4.66 us -> none  [local_by_channels(): query = short_rows(raw[0], taps[0]).astype(jnp.bfloat16)]
  transfers between devices with their start and end apart: 2 -> 0, of which waited for: 2 -> 0; matrix products, arithmetic and copies ran while one was open for 5% -> 0% of each run, Pallas kernels for 0% -> 0%
where the time goes in v2:
time: 286 us; the launch traced here: 285 us
  Pallas kernels  185 us (65%)
  matrix products  33.8 us (12%)
  blocking collectives  29.5 us (10%)
  local copies, waits for them, and re-layouts  19 us (7%)
  other arithmetic  17.6 us (6%)
    pallas_call x1, Pallas kernels, exchanged(): pl.pallas_call(functools.partial(exchange_kernel, count), out_shape=(jax....  185 us
    all_to_all x1, blocking collectives, local_by_channels(): lax.all_to_all(result, 'tok', split_axis=0, concat_axis=1, tiled=True)  29.5 us
    dot_general x1, matrix products, local_by_channels(): raw = jnp.dot(gathered, columns, preferred_element_type=jnp.float32)  22.2 us
    dot_general x6, matrix products, mul16(): jnp.einsum(spec, a.astype(jnp.bfloat16), b.astype(jnp.bfloat16), preferre...  11.5 us
    unnamed x13, local copies, waits for them, and re-layouts  6.47 us

profile of v2, /device:TPU:0, one launch (start us, length us, event | category | flops | bytes accessed | tf_op | source)
XLA Modules:
  0.0 285.2 jit_solution(2927474031541257200)
XLA Ops:
  1.1 2.4 copy.22
  3.4 1.3 copy.21
  4.7 1.3 copy.20
  6.0 2.2 pad_maximum_fusion
  8.2 2.8 copy.23.w_ref
  11.0 185.2 %shard_map.73 = (bf16[32,128,4096]{2,1,0:T(8,128)(2,1)}, bf16[32,128,384]{2,1,0:T(8,128)(2,1)}) custom-call(bf16[128,4096]{1,0:T(8,128)(2,1)} %tok_ref.1, bf16[32,128,384]{2,1,0:T(8,128)(2,1)} %copy.23.w_ref), custom_call_target="tpu_custom_call" | custom-call | tf_op jit(solution)/shard_map/pallas_call | solution.py:338
  196.2 22.2 %fusion.62 = f32[4096,384]{1,0:T(8,128)S(1)} fusion(bf16[4096,4096]{1,0:T(8,128)(2,1)} %bitcast.167, bf16[4096,384]{1,0:T(8,128)(2,1)} %bitcast.168), kind=kOutput, calls=%fused_computation.114 | convolution fusion | flops 12884901888 | bytes 42991616 | tf_op jit(solution)/shard_map/dot_general | solution.py:380
  218.4 2.4 fusion.61
  221.8 4.2 %multiply_convert_fusion.2 = bf16[4096,128]{1,0:T(8,128)(2,1)S(1)} fusion(f32[4096,128]{1,0:T(8,128)} %get-tuple-element.12, f32[4096,128]{1,0:T(8,128)S(1)} %get-tuple-element.11, f32[128]{0:T(128)S(1)} %get-tuple-element.28, f32[128]{0:T(128)S(1)} %get-tuple-element.21, f32[128]{0:T(128)S(1)} %get-tuple-element.22, f32[128]{0:T(128)S(1)} %get-tuple-element.23, ...), kind=kLoop, calls=%fused_computation.35 | loop fusion | flops 6291456 | bytes 5245952 | tf_op jit(solution)/shard_map/convert_element_type | solution.py:384
  226.0 1.3 reshape.218
  227.3 4.0 %fusion.16 = f32[64,2,64,128]{3,0,2,1:T(8,128)} fusion(bf16[64,1,64]{2,0,1:T(8,128)(2,1)S(1)} %get-tuple-element.34, bf16[64,1,64]{2,0,1:T(8,128)(2,1)S(1)} %get-tuple-element.33, bf16[64,8192]{1,0:T(8,128)(2,1)} %reshape.218), kind=kOutput, calls=%fused_computation.45 | convolution fusion | flops 134250496 | bytes 5259264 | tf_op jit(solution)/shard_map/kn,nc->kc/dot_general | solution.py:157
  231.7 1.2 fusion.11
  232.9 1.6 copy.30
  235.7 1.5 copy-done
  237.2 1.9 add_convert_fusion.4
  239.5 1.6 fusion.7
  241.2 1.6 fusion.9
  242.8 1.1 fusion.12
  244.7 1.4 subtract_convert_fusion
  246.3 2.8 fusion
  249.1 1.7 reshape.222
  250.8 3.8 %multiply_convert_fusion = bf16[4096,128]{1,0:T(8,128)(2,1)S(1)} fusion(f32[4096,128]{1,0:T(8,128)} %get-tuple-element.13, f32[4096,128]{1,0:T(8,128)S(1)} %reshape.222, bf16[4096,128]{1,0:T(8,128)(2,1)S(1)} %multiply_convert_fusion.2, f32[128]{0:T(128)S(1)} %copy-done.4, f32[128]{0:T(128)S(1)} %get-tuple-element.26, f32[128]{0:T(128)S(1)} %get-tuple-element.27, ...), kind=kLoop, calls=%fused_computation.23 | loop fusion | flops 7340032 | bytes 6293504 | tf_op jit(solution)/shard_map/convert_element_type | solution.py:389
  254.6 29.5 %all_to_all.19 = bf16[32,128,128]{2,1,0:T(8,128)(2,1)S(1)} all-to-all(bf16[32,128,128]{2,1,0:T(8,128)(2,1)S(1)} %bitcast.162), channel_id=1, replica_groups=mesh['tok'=32,'tp'=1] {'tok'}, dimensions={0} | all-to-all | bytes 2097152 | tf_op jit(solution)/shard_map/all_to_all | solution.py:390
  284.1 1.1 copy_bitcast_fusion
  (28 shorter events, 4.9 us)
Async XLA Ops:
  0.0 3.4 %copy-start.2 = (bf16[128,4096]{1,0:T(8,128)(2,1)S(1)}, bf16[128,4096]{1,0:T(8,128)(2,1)}, u32[]{:S(2)}) copy-start(bf16[128,4096]{1,0:T(8,128)(2,1)} %param.9) | copy-start | bytes 3145732
  1.0 3.7 %copy-start.3 = (bf16[128,4096]{1,0:T(8,128)(2,1)S(1)}, bf16[128,4096]{1,0:T(8,128)(2,1)}, u32[]{:S(2)}) copy-start(bf16[128,4096]{1,0:T(8,128)(2,1)} %param.8) | copy-start | bytes 3145732
  227.3 4.2 %copy-start.1 = (f32[128,4096]{1,0:T(8,128)S(1)}, f32[128,4096]{1,0:T(8,128)}, u32[]{:S(2)}) copy-start(f32[128,4096]{1,0:T(8,128)} %param.12) | copy-start | bytes 6291460
  235.0 2.2 copy-start
  249.1 1.7 copy-start.4

commit v3 on v2

--- a/solution.py
+++ b/solution.py
@@ -198,7 +198,21 @@
 
 
 def exchange_kernel(
-    count, tok_ref, w_ref, all_tok, all_w, send_sem, recv_sem, w_send, w_recv, local_sem
+    count,
+    tok_ref,
+    w_query,
+    w_key,
+    w_value,
+    raw_ref,
+    all_tok,
+    columns,
+    held,
+    send_sem,
+    recv_sem,
+    w_send,
+    w_recv,
+    local_sem,
+    held_sem,
 ):
     me = lax.axis_index("tok")
     depth = count // 8
@@ -220,9 +234,21 @@
     pl.semaphore_wait(barrier, count - 1)
 
     own_tok = pltpu.make_async_copy(tok_ref, all_tok.at[me], local_sem.at[0])
-    own_w = pltpu.make_async_copy(w_ref.at[me], all_w.at[me], local_sem.at[1])
     own_tok.start()
-    own_w.start()
+    weights = (w_query, w_key, w_value)
+    w_rows = w_query.shape[0]
+    w_cols = w_query.shape[1] // count
+
+    def w_ends(kind, dest):
+        src = weights[kind].at[:, pl.ds(pl.multiple_of(dest * w_cols, w_cols), w_cols)]
+        landing = pl.ds(pl.multiple_of(me * w_rows, w_rows), w_rows)
+        return src, columns.at[landing, pl.ds(kind * w_cols, w_cols)]
+
+    own_w = [
+        pltpu.make_async_copy(*w_ends(kind, me), local_sem.at[1 + kind]) for kind in range(3)
+    ]
+    for copy in own_w:
+        copy.start()
 
     def tok_copy(half, block, dest, slot, own=False):
         part = pl.ds(half * rows, rows)
@@ -260,18 +286,22 @@
         put(None, half, me, me + second, 3, own=True)
         put(None, half, me, me + step_core, 4, own=True)
 
-    def w_copy(j):
+    def w_copy(j, kind):
         dest = lax.rem(me + j, count)
+        src, dst = w_ends(kind, dest)
         return pltpu.make_async_remote_copy(
-            src_ref=w_ref.at[dest],
-            dst_ref=all_w.at[me],
-            send_sem=w_send.at[j],
-            recv_sem=w_recv.at[j],
+            src_ref=src,
+            dst_ref=dst,
+            send_sem=w_send.at[kind, j],
+            recv_sem=w_recv.at[kind, j],
             device_id={"tok": dest},
             device_id_type=pl.DeviceIdType.MESH,
         )
 
-    pl.loop(1, count)(lambda j: w_copy(j).start())
+    @pl.loop(1, count)
+    def _(j):
+        for kind in range(3):
+            w_copy(j, kind).start()
 
     def both_ways(distance):
         yield (z >= distance, -8 * distance)
@@ -302,19 +332,75 @@
                 put(cond, half, block, me + step_core, 4)
         from_first(distance - 1)
     from_first(depth - 1)
-    for distance in range(depth):
-        for half in range(2):
-            first, second = turns[half]
-            for cond, shift in both_ways(distance):
+    own_tok.wait()
+    for copy in own_w:
+        copy.wait()
+
+    @pl.loop(1, count)
+    def _(j):
+        for kind in range(3):
+            w_copy(j, kind).wait_recv()
+
+    def last_leg(turn):
+        distance = (turn + 1) // 2
+        there = z + distance * (1 - 2 * lax.rem(turn, 2))
+        return there, jnp.logical_and(there >= 0, there < depth)
+
+    def to_core(half, there, base):
+        block = there * 8 + lax.rem(me, 8) + base
+        return tok_copy(half, block, me + step_core, 4)
+
+    def load(there, k):
+        block = there * 8 + 2 * lax.rem(k, 4) + jnp.where(k < 4, core, 1 - core)
+        return block, pltpu.make_async_copy(all_tok.at[block], held.at[k], held_sem.at[k])
+
+    block_rows = tok_ref.shape[0]
+
+    @pl.loop(0, 2 * depth - 1)
+    def _(turn):
+        there, valid = last_leg(turn)
+
+        @pl.when(valid)
+        def _():
+            for half in range(2):
+                first, second = turns[half]
                 for base in (second, first + second):
-                    block = me + base + shift
-                    arrived(cond, half, block)
-                    put(cond, half, block, me + step_core, 4)
-
-    @pl.loop(0, count // 2)
-    def _(pair):
-        for half in range(2):
-            tok_copy(half, 2 * pair + 1 - core, me, 0).wait_recv()
+                    to_core(half, there, base).wait_recv()
+                    to_core(half, there, base).start()
+
+            @pl.loop(0, 4)
+            def _(k):
+                load(there, k)[1].start()
+
+            @pl.loop(0, 8)
+            def _(k):
+                block, copy = load(there, k)
+
+                @pl.when(k == 1)
+                def _():
+                    @pl.loop(0, 4)
+                    def _(other):
+                        later, later_copy = load(there, other + 4)
+                        for half in range(2):
+                            tok_copy(half, later, me, 0).wait_recv()
+                        later_copy.start()
+
+                copy.wait()
+                place = pl.ds(pl.multiple_of(block * block_rows, block_rows), block_rows)
+                raw_ref[place, :] = jnp.dot(
+                    held[k], columns[...], preferred_element_type=jnp.float32
+                )
+
+    @pl.loop(0, 2 * depth - 1)
+    def _(turn):
+        there, valid = last_leg(turn)
+
+        @pl.when(valid)
+        def _():
+            for half in range(2):
+                first, second = turns[half]
+                for base in (second, first + second):
+                    to_core(half, there, base).wait_send()
 
     for cond, half, block, dest, slot in sent:
 
@@ -325,47 +411,55 @@
 
     @pl.loop(1, count)
     def _(j):
-        w_copy(j).wait_recv()
-        w_copy(j).wait_send()
-
-    own_tok.wait()
-    own_w.wait()
+        for kind in range(3):
+            w_copy(j, kind).wait_send()
 
 
 def exchanged(tokens, weights):
     count = lax.axis_size("tok")
+    rows, width = tokens.shape
+    w_rows, channels = weights[0].shape
+    cols = 3 * channels // count
     anywhere = pl.BlockSpec(memory_space=pl.ANY)
-    return pl.pallas_call(
+    raw, _ = pl.pallas_call(
         functools.partial(exchange_kernel, count),
         out_shape=(
-            jax.ShapeDtypeStruct((count,) + tokens.shape, tokens.dtype),
-            jax.ShapeDtypeStruct(weights.shape, weights.dtype),
+            jax.ShapeDtypeStruct((count * rows, cols), jnp.float32),
+            jax.ShapeDtypeStruct((count, rows, width), tokens.dtype),
         ),
-        in_specs=[anywhere, anywhere],
-        out_specs=(anywhere, anywhere),
+        in_specs=[anywhere] * 4,
+        out_specs=(pl.BlockSpec(memory_space=pltpu.VMEM), anywhere),
         scratch_shapes=[
+            pltpu.VMEM((count * w_rows, cols), weights[0].dtype),
+            pltpu.VMEM((8, rows, width), tokens.dtype),
             pltpu.SemaphoreType.DMA((2, count // 2, 5)),
             pltpu.SemaphoreType.DMA((2, count)),
-            pltpu.SemaphoreType.DMA((count,)),
-            pltpu.SemaphoreType.DMA((count,)),
-            pltpu.SemaphoreType.DMA((2,)),
+            pltpu.SemaphoreType.DMA((3, count)),
+            pltpu.SemaphoreType.DMA((3, count)),
+            pltpu.SemaphoreType.DMA((4,)),
+            pltpu.SemaphoreType.DMA((8,)),
         ],
-        compiler_params=pltpu.CompilerParams(collective_id=0, has_side_effects=True),
-    )(tokens, weights)
-
-
-def gathered_and_columns(tokens, weights):
+        compiler_params=pltpu.CompilerParams(
+            collective_id=0, has_side_effects=True, vmem_limit_bytes=40 * 2**20
+        ),
+    )(tokens, *weights)
+    return raw
+
+
+def projected(tokens, weights):
     count = lax.axis_size("tok")
-    kinds, depth, channels = weights.shape
-    blocks = weights.reshape(kinds, depth, count, channels // count)
-    blocks = blocks.transpose(2, 1, 0, 3).reshape(count, depth, kinds * channels // count)
-    if count % 8 == 0 and tokens.shape[0] % 32 == 0:
-        all_tokens, columns = exchanged(tokens, blocks)
-        all_tokens = all_tokens.reshape(count * tokens.shape[0], tokens.shape[1])
-    else:
-        all_tokens = lax.all_gather(tokens, "tok", axis=0, tiled=True)
-        columns = lax.all_to_all(blocks, "tok", split_axis=0, concat_axis=0, tiled=True)
-    return all_tokens, columns.reshape(count * depth, kinds * channels // count)
+    rows = tokens.shape[0]
+    w_rows, channels = weights[0].shape
+    if count % 8 == 0 and rows % 32 == 0 and w_rows % 16 == 0 and channels % (128 * count) == 0:
+        return exchanged(tokens, weights)
+    gathered = lax.all_gather(tokens, "tok", axis=0, tiled=True)
+    columns = [
+        lax.all_to_all(weight, "tok", split_axis=1, concat_axis=0, tiled=True)
+        for weight in weights
+    ]
+    return jnp.dot(
+        gathered, jnp.concatenate(columns, axis=1), preferred_element_type=jnp.float32
+    )
 
 
 def short_rows(raw, taps):
@@ -376,8 +470,7 @@
 def local_by_channels(tokens, w_query, w_key, w_value, short_taps, filters, skip_gain):
     owned = filters.shape[0]
     start = lax.axis_index("tok") * owned
-    gathered, columns = gathered_and_columns(tokens, jnp.stack([w_query, w_key, w_value]))
-    raw = jnp.dot(gathered, columns, preferred_element_type=jnp.float32)
+    raw = projected(tokens, (w_query, w_key, w_value))
     raw = [raw[:, kind * owned : (kind + 1) * owned] for kind in range(3)]
     taps = lax.dynamic_slice_in_dim(short_taps, start, owned, axis=2)
     query = short_rows(raw[0], taps[0]).astype(jnp.bfloat16)

time: 286 us -> 271 us (0.948)
  matrix products: 33.8 us -> 11.5 us
  Pallas kernels: 185 us -> 199 us
  local copies, waits for them, and re-layouts: 19 us -> 16.1 us
    dot_general x1 -> x0, matrix products: 22.2 us -> none  [local_by_channels(): raw = jnp.dot(gathered, columns, preferred_element_type=jnp.float32)]
    pallas_call x1, Pallas kernels: 185 us -> 199 us  [exchanged(): pl.pallas_call(functools.partial(exchange_kernel, count), out_shape=(jax....]
    another operation x5 -> x4, other arithmetic: 5.8 us -> 3.62 us
    unnamed x13 -> x14, local copies, waits for them, and re-layouts: 6.47 us -> 6.4 us
where the time goes in v3:
time: 271 us
  Pallas kernels  199 us (73%)
  blocking collectives  28 us (10%)
  local copies, waits for them, and re-layouts  16.1 us (6%)
  other arithmetic  15.4 us (6%)
  matrix products  11.5 us (4%)
    pallas_call x1, Pallas kernels, exchanged(): pl.pallas_call(functools.partial(exchange_kernel, count), out_shape=(jax....  199 us
    all_to_all x1, blocking collectives, local_by_channels(): lax.all_to_all(result, 'tok', split_axis=0, concat_axis=1, tiled=True)  28 us
    dot_general x6, matrix products, mul16(): jnp.einsum(spec, a.astype(jnp.bfloat16), b.astype(jnp.bfloat16), preferre...  11.5 us
    unnamed x14, local copies, waits for them, and re-layouts  6.4 us

profile of v3, /device:TPU:0, one launch (start us, length us, event | category | flops | bytes accessed | tf_op | source)
XLA Modules:
  0.0 270.5 jit_solution(18318083871066905471)
XLA Ops:
  1.1 1.2 copy-done
  2.3 1.2 copy-done.1
  3.5 1.2 copy-done.2
  4.7 1.2 copy-done.3
  5.9 199.2 %shard_map.73 = (f32[4096,384]{1,0:T(8,128)S(1)}, bf16[32,128,4096]{2,1,0:T(8,128)(2,1)}) custom-call(bf16[128,4096]{1,0:T(8,128)(2,1)S(1)} %copy-done, bf16[128,4096]{1,0:T(8,128)(2,1)S(1)} %copy-done.1, bf16[128,4096]{1,0:T(8,128)(2,1)S(1)} %copy-done.2, bf16[128,4096]{1,0:T(8,128)(2,1)S(1)} %copy-done.3), custom_call_target="tpu_custom_call" | custom-call | tf_op jit(solution)/shard_map/pallas_call | solution.py:424
  205.1 2.4 fusion.61
  207.6 0.9 fusion.52
  208.5 4.2 %multiply_convert_fusion.2 = bf16[4096,128]{1,0:T(8,128)(2,1)S(1)} fusion(f32[4096,128]{1,0:T(8,128)} %get-tuple-element.10, f32[4096,128]{1,0:T(8,128)S(1)} %get-tuple-element.9, f32[128]{0:T(128)S(1)} %get-tuple-element.26, f32[128]{0:T(128)S(1)} %get-tuple-element.19, f32[128]{0:T(128)S(1)} %get-tuple-element.20, f32[128]{0:T(128)S(1)} %get-tuple-element.21, ...), kind=kLoop, calls=%fused_computation.34 | loop fusion | flops 6291456 | bytes 5245952 | tf_op jit(solution)/shard_map/convert_element_type | solution.py:477
  212.7 1.3 reshape.199
  214.0 4.0 %fusion.16 = f32[64,2,64,128]{3,0,2,1:T(8,128)} fusion(bf16[64,1,64]{2,0,1:T(8,128)(2,1)S(1)} %get-tuple-element.32, bf16[64,1,64]{2,0,1:T(8,128)(2,1)S(1)} %get-tuple-element.31, bf16[64,8192]{1,0:T(8,128)(2,1)} %reshape.199), kind=kOutput, calls=%fused_computation.44 | convolution fusion | flops 134250496 | bytes 5259264 | tf_op jit(solution)/shard_map/kn,nc->kc/dot_general | solution.py:157
  218.4 1.2 fusion.11
  219.6 1.6 copy.23
  222.4 1.5 copy-done.4
  223.9 1.8 add_convert_fusion.4
  226.1 1.6 fusion.7
  227.7 1.6 fusion.9
  229.4 1.1 fusion.12
  230.4 0.8 fusion.3
  231.2 1.6 subtract_convert_fusion
  233.0 2.8 %fusion = f32[64,8192]{1,0:T(8,128)} fusion(bf16[128,64]{1,0:T(8,128)(2,1)S(1)} %bitcast.152, bf16[16,8,64,128]{3,2,1,0:T(8,128)(2,1)S(1)} %bitcast.150), kind=kOutput, calls=%fused_computation | convolution fusion | flops 134217728 | bytes 4210688 | tf_op jit(solution)/shard_map/nk,kc->nc/dot_general | solution.py:157
  235.8 1.7 reshape.203
  237.5 3.8 %multiply_convert_fusion = bf16[4096,128]{1,0:T(8,128)(2,1)S(1)} fusion(f32[4096,128]{1,0:T(8,128)} %get-tuple-element.11, f32[4096,128]{1,0:T(8,128)S(1)} %reshape.203, bf16[4096,128]{1,0:T(8,128)(2,1)S(1)} %multiply_convert_fusion.2, f32[128]{0:T(128)S(1)} %copy-done.6, f32[128]{0:T(128)S(1)} %get-tuple-element.24, f32[128]{0:T(128)S(1)} %get-tuple-element.25, ...), kind=kLoop, calls=%fused_computation.22 | loop fusion | flops 7340032 | bytes 6293504 | tf_op jit(solution)/shard_map/convert_element_type | solution.py:482
  241.3 28.0 %all_to_all.19 = bf16[32,128,128]{2,1,0:T(8,128)(2,1)S(1)} all-to-all(bf16[32,128,128]{2,1,0:T(8,128)(2,1)S(1)} %bitcast.151), channel_id=1, replica_groups=mesh['tok'=32,'tp'=1] {'tok'}, dimensions={0} | all-to-all | bytes 2097152 | tf_op jit(solution)/shard_map/all_to_all | solution.py:483
  269.4 1.1 copy_bitcast_fusion
  (26 shorter events, 3.2 us)
Async XLA Ops:
  1.0 1.2 copy-start
  2.3 1.2 copy-start.1
  3.5 1.2 copy-start.2
  4.7 1.2 copy-start.3
  214.0 4.2 %copy-start.5 = (f32[128,4096]{1,0:T(8,128)S(1)}, f32[128,4096]{1,0:T(8,128)}, u32[]{:S(2)}) copy-start(f32[128,4096]{1,0:T(8,128)} %param.12) | copy-start | bytes 6291460
  221.7 2.2 copy-start.4
  235.8 1.7 copy-start.6

commit v4 on v3

--- a/solution.py
+++ b/solution.py
@@ -298,10 +298,16 @@
             device_id_type=pl.DeviceIdType.MESH,
         )
 
-    @pl.loop(1, count)
-    def _(j):
-        for kind in range(3):
-            w_copy(j, kind).start()
+    def send_weights(distance):
+        kinds = [kind for kind in range(3) if min(1 + kind // 2, depth - 1) == distance]
+        if kinds:
+
+            @pl.loop(1, count)
+            def _(j):
+                for kind in kinds:
+                    w_copy(j, kind).start()
+
+    send_weights(0)
 
     def both_ways(distance):
         yield (z >= distance, -8 * distance)
@@ -330,6 +336,7 @@
                 put(cond, half, block, me + first, 2)
                 put(cond, half, block, me + second, 3)
                 put(cond, half, block, me + step_core, 4)
+        send_weights(distance)
         from_first(distance - 1)
     from_first(depth - 1)
     own_tok.wait()

time: 271 us -> 269 us (level)
  no operation moved by 1% of the time
where the time goes in v4:
time: 269 us
  Pallas kernels  197 us (73%)
  blocking collectives  28.1 us (10%)
  local copies, waits for them, and re-layouts  16.1 us (6%)
  other arithmetic  15.4 us (6%)
  matrix products  11.5 us (4%)
    pallas_call x1, Pallas kernels, exchanged(): pl.pallas_call(functools.partial(exchange_kernel, count), out_shape=(jax....  197 us
    all_to_all x1, blocking collectives, local_by_channels(): lax.all_to_all(result, 'tok', split_axis=0, concat_axis=1, tiled=True)  28.1 us
    dot_general x6, matrix products, mul16(): jnp.einsum(spec, a.astype(jnp.bfloat16), b.astype(jnp.bfloat16), preferre...  11.5 us
    unnamed x14, local copies, waits for them, and re-layouts  6.4 us

profile of v4, /device:TPU:0, one launch (start us, length us, event | category | flops | bytes accessed | tf_op | source)
XLA Modules:
  0.0 268.9 jit_solution(1445631492854630068)
XLA Ops:
  1.1 1.2 copy-done
  2.3 1.2 copy-done.1
  3.5 1.2 copy-done.2
  4.7 1.2 copy-done.3
  5.9 197.5 %shard_map.73 = (f32[4096,384]{1,0:T(8,128)S(1)}, bf16[32,128,4096]{2,1,0:T(8,128)(2,1)}) custom-call(bf16[128,4096]{1,0:T(8,128)(2,1)S(1)} %copy-done, bf16[128,4096]{1,0:T(8,128)(2,1)S(1)} %copy-done.1, bf16[128,4096]{1,0:T(8,128)(2,1)S(1)} %copy-done.2, bf16[128,4096]{1,0:T(8,128)(2,1)S(1)} %copy-done.3), custom_call_target="tpu_custom_call" | custom-call | tf_op jit(solution)/shard_map/pallas_call | solution.py:431
  203.4 2.4 fusion.61
  205.9 0.9 fusion.52
  206.8 4.2 %multiply_convert_fusion.2 = bf16[4096,128]{1,0:T(8,128)(2,1)S(1)} fusion(f32[4096,128]{1,0:T(8,128)} %get-tuple-element.10, f32[4096,128]{1,0:T(8,128)S(1)} %get-tuple-element.9, f32[128]{0:T(128)S(1)} %get-tuple-element.26, f32[128]{0:T(128)S(1)} %get-tuple-element.19, f32[128]{0:T(128)S(1)} %get-tuple-element.20, f32[128]{0:T(128)S(1)} %get-tuple-element.21, ...), kind=kLoop, calls=%fused_computation.34 | loop fusion | flops 6291456 | bytes 5245952 | tf_op jit(solution)/shard_map/convert_element_type | solution.py:484
  211.0 1.3 reshape.199
  212.3 4.0 %fusion.16 = f32[64,2,64,128]{3,0,2,1:T(8,128)} fusion(bf16[64,1,64]{2,0,1:T(8,128)(2,1)S(1)} %get-tuple-element.32, bf16[64,1,64]{2,0,1:T(8,128)(2,1)S(1)} %get-tuple-element.31, bf16[64,8192]{1,0:T(8,128)(2,1)} %reshape.199), kind=kOutput, calls=%fused_computation.44 | convolution fusion | flops 134250496 | bytes 5259264 | tf_op jit(solution)/shard_map/kn,nc->kc/dot_general | solution.py:157
  216.7 1.2 fusion.11
  217.9 1.6 copy.23
  220.7 1.5 copy-done.4
  222.2 1.8 add_convert_fusion.4
  224.4 1.6 fusion.7
  226.0 1.6 fusion.9
  227.7 1.1 fusion.12
  228.7 0.8 fusion.3
  229.5 1.6 subtract_convert_fusion
  231.3 2.8 %fusion = f32[64,8192]{1,0:T(8,128)} fusion(bf16[128,64]{1,0:T(8,128)(2,1)S(1)} %bitcast.152, bf16[16,8,64,128]{3,2,1,0:T(8,128)(2,1)S(1)} %bitcast.150), kind=kOutput, calls=%fused_computation | convolution fusion | flops 134217728 | bytes 4210688 | tf_op jit(solution)/shard_map/nk,kc->nc/dot_general | solution.py:157
  234.1 1.7 reshape.203
  235.8 3.8 %multiply_convert_fusion = bf16[4096,128]{1,0:T(8,128)(2,1)S(1)} fusion(f32[4096,128]{1,0:T(8,128)} %get-tuple-element.11, f32[4096,128]{1,0:T(8,128)S(1)} %reshape.203, bf16[4096,128]{1,0:T(8,128)(2,1)S(1)} %multiply_convert_fusion.2, f32[128]{0:T(128)S(1)} %copy-done.6, f32[128]{0:T(128)S(1)} %get-tuple-element.24, f32[128]{0:T(128)S(1)} %get-tuple-element.25, ...), kind=kLoop, calls=%fused_computation.22 | loop fusion | flops 7340032 | bytes 6293504 | tf_op jit(solution)/shard_map/convert_element_type | solution.py:489
  239.7 28.1 %all_to_all.19 = bf16[32,128,128]{2,1,0:T(8,128)(2,1)S(1)} all-to-all(bf16[32,128,128]{2,1,0:T(8,128)(2,1)S(1)} %bitcast.151), channel_id=1, replica_groups=mesh['tok'=32,'tp'=1] {'tok'}, dimensions={0} | all-to-all | bytes 2097152 | tf_op jit(solution)/shard_map/all_to_all | solution.py:490
  267.7 1.1 copy_bitcast_fusion
  (26 shorter events, 3.2 us)
Async XLA Ops:
  1.0 1.2 copy-start
  2.3 1.2 copy-start.1
  3.5 1.2 copy-start.2
  4.7 1.2 copy-start.3
  212.3 4.2 %copy-start.5 = (f32[128,4096]{1,0:T(8,128)S(1)}, f32[128,4096]{1,0:T(8,128)}, u32[]{:S(2)}) copy-start(f32[128,4096]{1,0:T(8,128)} %param.12) | copy-start | bytes 6291460
  220.0 2.2 copy-start.4
  234.1 1.7 copy-start.6
